TPU v7x, 256 devices: a whole 4x4x8 slice. The times are simulated.
256 devices in a mesh: seq: 64 (over y, z, core), fsdp: 4 (over x).
Axes of the slice: x: 4, y: 4, z: 8, core: 2. Of those that a mesh axis runs over, the one named last changes fastest.
Arguments:
- tokens: bfloat16 [65536, 4096], P('seq', 'fsdp'), may hold values from -6 to 6
- projection: bfloat16 [3, 4096, 2048], P(None, 'seq', 'fsdp'), may hold values from -0.09375 to 0.09375
- log_decay: float32 [65536, 16], P('seq', 'fsdp'), may hold values from -2 to 0, as said below
Outputs:
- attended: bfloat16 [65536, 2048], P('seq', 'fsdp')
Inputs may be any that keep to these rules, and one draw needn't show every extreme that they name: `log_decay`: negative logarithms of decay factors, one for each position and head.
All inputs are finite; a program needn't handle non-finite values.
Results may differ from a plain program's by a relative error of at most 0.006.
Values may be sent and summed in bfloat16 or wider, within the bound.
No kernel may reach another device: no remote copies, remote signals or barrier semaphores. Data moves between devices by JAX's collectives and lax.ppermute only.
A program may use at most 64 MiB of HBM per device.

v0:
```python
import jax
import jax.numpy as jnp
from jax import lax
from jax.sharding import PartitionSpec as P

BLK = 512


def entering(part, axis, combine, identity):
    place = lax.axis_index(axis)
    gathered = jax.tree.map(lambda a: lax.all_gather(a, axis), part)
    state = jax.tree.map(lambda a, e: jnp.zeros_like(a) + jnp.asarray(e, a.dtype), part, identity)

    def one(hop, state):
        return combine(
            state, jax.tree.map(lambda a: lax.dynamic_index_in_dim(a, hop, 0, False), gathered)
        )

    return lax.fori_loop(0, place, one, state)


def local_states(key_vecs, value_vecs, decay):
    running = jnp.cumsum(decay, axis=1)
    last = running[:, -1]
    carried = key_vecs.astype(jnp.float32) * jnp.exp(last[:, None, :] - running)[..., None]
    fresh = jnp.einsum(
        "nshd,nshe->nhde", carried, value_vecs.astype(jnp.float32), precision=lax.Precision.HIGHEST
    )

    def advance(state, inputs):
        block_last, block_fresh = inputs
        return (jnp.exp(block_last)[:, None, None] * state + block_fresh, state)

    start = jnp.zeros(fresh.shape[1:], jnp.float32)
    final, before = lax.scan(advance, start, (last, fresh))
    leading = jnp.cumsum(last, axis=0) - last
    whole_decay = jnp.exp(jnp.sum(last, axis=0))
    return (final, before, leading, whole_decay)


def combine(earlier, later):
    return (earlier[0] * later[0], later[0][:, None, None] * earlier[1] + later[1])


def chain(key_raw, value_raw, decay, shaped):
    key_vecs = shaped(jax.nn.silu(key_raw).astype(jnp.bfloat16))
    value_vecs = shaped(value_raw.astype(jnp.bfloat16))
    final, before, leading, whole_decay = local_states(key_vecs, value_vecs, decay)
    identity = (jnp.ones_like(whole_decay), jnp.zeros_like(final))
    carry = entering((whole_decay, final), "seq", combine, identity)
    incoming = before + jnp.exp(leading)[:, :, None, None] * carry[1][None]
    return (key_vecs, value_vecs, incoming)


def attend_block(inputs):
    queries, key_vecs, value_vecs, decay, state = inputs
    running = jnp.cumsum(decay, axis=0)
    across = running.T
    gap = across[:, :, None] - across[:, None, :]
    lower = jnp.arange(gap.shape[1])[:, None] >= jnp.arange(gap.shape[2])[None, :]
    fading = jnp.exp(jnp.where(lower[None], gap, -1e30))
    scores = jnp.einsum("thd,shd->hts", queries, key_vecs, preferred_element_type=jnp.float32)
    weights = (fading * scores).astype(jnp.bfloat16)
    intra = jnp.einsum("hts,she->the", weights, value_vecs, preferred_element_type=jnp.float32)
    inter = jnp.exp(running)[:, :, None] * jnp.einsum(
        "thd,hde->the", queries.astype(jnp.float32), state, precision=lax.Precision.HIGHEST
    )
    mixed = intra + inter
    normed = mixed * lax.rsqrt(jnp.mean(mixed * mixed, axis=-1, keepdims=True) + 1e-06)
    return normed.astype(jnp.bfloat16)


def on_device(tokens, projection, log_decay):
    features = lax.all_gather(tokens, "fsdp", axis=1, tiled=True)
    rows = features.shape[0]
    heads = log_decay.shape[1]
    width = projection.shape[2]
    head = width // heads
    blocks = rows // BLK

    def shaped(matrix):
        return matrix.reshape(blocks, BLK, heads, head)

    decay = log_decay.reshape(blocks, BLK, heads)
    raw = jnp.einsum(
        "td,cdn->ctn",
        features,
        lax.all_gather(projection, "seq", axis=1, tiled=True),
        preferred_element_type=jnp.float32,
    )
    key_vecs, value_vecs, incoming = chain(raw[1], raw[2], decay, shaped)
    query_raw = raw[0]
    queries = shaped(jax.nn.silu(query_raw).astype(jnp.bfloat16))
    outputs = lax.map(attend_block, (queries, key_vecs, value_vecs, decay, incoming))
    return outputs.reshape(rows, width)


def solution(mesh):
    in_specs = (P("seq", "fsdp"), P(None, "seq", "fsdp"), P("seq", "fsdp"))
    out_specs = P("seq", "fsdp")
    return jax.shard_map(
        on_device, mesh=mesh, in_specs=in_specs, out_specs=out_specs, check_vma=False
    )
```

profile of v0, /device:TPU:249, one launch (start us, length us, event | category | flops | bytes accessed | tf_op | source)
XLA Modules:
  0.0 447.1 jit_solution(9601108571453135276)
XLA Ops:
  8.1 2.4 reduce-window.14
  11.5 83.5 %all-gather.8.cloned.1.call-done = bf16[1024,4096]{1,0:T(8,128)(2,1)} async-done(((bf16[1024,1024]{1,0:T(8,128)(2,1)}), bf16[1024,4096]{1,0:T(8,128)(2,1)}) %all-gather.8.cloned.1.call-update) | async-done | bytes 8388624 | tf_op jit(solution)/shard_map/all_gather | solution.py:74
  95.0 90.9 %all-gather.6.cloned.1.call-done = bf16[3,4096,512]{2,1,0:T(8,128)(2,1)} async-done(((bf16[3,64,512]{2,1,0:T(8,128)(2,1)}), bf16[3,4096,512]{2,1,0:T(8,128)(2,1)}) %all-gather.6.cloned.1.call-update) | async-done | bytes 12582928 | tf_op jit(solution)/shard_map/all_gather | solution.py:88
  185.9 17.3 %fusion.27 = f32[3,1024,512]{1,2,0:T(8,128)S(1)} fusion(bf16[3,4096,512]{2,1,0:T(8,128)(2,1)} %all-gather.6.cloned.1.call-done, bf16[1024,4096]{1,0:T(8,128)(2,1)} %all-gather.8.cloned.1.call-done), kind=kOutput, calls=%fused_computation.39 | convolution fusion | flops 12884901888 | bytes 27262976 | tf_op jit(solution)/shard_map/td,cdn->ctn/dot_general | solution.py:85
  203.3 1.8 fusion.35
  205.1 1.6 convert_element_type.24
  206.7 2.8 squeeze.42
  209.4 2.8 copy.51
  212.2 4.0 squeeze.41
  216.2 4.1 copy.49
  220.3 2.8 multiply_convert_fusion.2
  223.1 2.7 fusion.30
  228.3 124.5 %all-reduce = f32[256]{0:T(256)S(1)} all-reduce(f32[256]{0:T(256)S(1)} %exponential_dynamic-update-slice_fusion), channel_id=2, replica_groups=mesh['seq'=64,'fsdp'=4] {'seq'}, use_global_device_ids=true, to_apply=%add | all-reduce | flops 256 | bytes 2048
  353.0 1.2 copy.54
  354.2 69.7 %while.35 = (s32[]{:T(128)}, f32[4,128,128]{2,1,0:T(8,128)S(1)}, s32[]{:T(128)}, f32[64,4]{1,0:T(8,128)S(1)}, f32[64,4,128,128]{3,2,1,0:T(8,128)}, /*index=5*/s32[]{:T(128)}, s32[]{:T(128)}, s32[]{:T(128)}) while((s32[]{:T(128)}, f32[4,128,128]{2,1,0:T(8,128)S(1)}, s32[]{:T(128)}, f32[64,4]{1,0:T(8,128)S(1)}, f32[64,4,128,128]{3,2,1,0:T(8,128)}, ...), condition=%wide.region_7.8_spmd, body=%wide.region_6.7_spmd.sunk | while | flops 131077 | bytes 786615 | solution.py:19
  354.2 1.1 bitcast_add_fusion.4
  355.3 1.1 bitcast_add_fusion.4
  356.4 1.1 bitcast_add_fusion.4
  357.5 1.1 bitcast_add_fusion.4
  358.6 1.1 bitcast_add_fusion.4
  359.7 1.1 bitcast_add_fusion.4
  364.1 1.1 bitcast_add_fusion.4
  365.2 1.1 bitcast_add_fusion.4
  366.3 1.1 bitcast_add_fusion.4
  367.4 1.1 bitcast_add_fusion.4
  368.5 1.1 bitcast_add_fusion.4
  369.6 1.1 bitcast_add_fusion.4
  375.2 1.1 bitcast_add_fusion.4
  376.3 1.1 bitcast_add_fusion.4
  377.4 1.1 bitcast_add_fusion.4
  378.5 1.1 bitcast_add_fusion.4
  379.6 1.1 bitcast_add_fusion.4
  380.7 1.1 bitcast_add_fusion.4
  385.1 1.1 bitcast_add_fusion.4
  386.2 1.1 bitcast_add_fusion.4
  387.3 1.1 bitcast_add_fusion.4
  388.4 1.1 bitcast_add_fusion.4
  389.5 1.1 bitcast_add_fusion.4
  390.6 1.1 bitcast_add_fusion.4
  396.1 1.1 bitcast_add_fusion.4
  397.2 1.1 bitcast_add_fusion.4
  398.3 1.1 bitcast_add_fusion.4
  424.0 14.2 %while.36 = (s32[]{:T(128)}, bf16[2,512,4,128]{3,2,1,0:T(4,128)(2,1)}, bf16[2,512,4,128]{1,3,2,0:T(8,128)(2,1)}, f32[2,512,4]{1,2,0:T(4,128)S(1)}, bf16[2,512,4,...) while((s32[]{:T(128)}, ...), condition=%wide.region_12.13_spmd, body=%wide.region_8.12_spmd.sunk | while | flops 945817664 | bytes 9857989 | solution.py:94
  424.0 1.2 reduce-window.24
  425.8 3.1 fusion.46
  431.1 1.2 reduce-window.24
  432.9 3.1 fusion.46
  438.2 2.4 copy.70
  (172 shorter events, 49.3 us)
Async XLA Ops:
  6.5 1.5 copy-start.5
  6.5 88.4 %all-gather.8.cloned.1.call-start = ((), (), s32[]{:S(2)}) async-start(), calls=%async_computation.1 | async-start | bytes 10485760 | tf_op jit(solution)/shard_map/all_gather | solution.py:74
  7.3 178.6 %all-gather.6.cloned.1.call-start = ((), (), s32[]{:S(2)}) async-start(), calls=%async_computation | async-start | bytes 12779520 | tf_op jit(solution)/shard_map/all_gather | solution.py:88
  8.0 346.1 %all-gather.10.cloned.1.call-start = ((), (), s32[]{:S(2)}) async-start(), calls=%async_computation.2 | async-start | bytes 17039360 | tf_op jit(solution)/shard_map/all_gather | solution.py:11
  220.3 2.8 copy-start.1
  223.1 2.8 copy-start.3
  223.1 2.8 copy-start.4
  225.9 1.2 copy-start.6
  225.9 127.1 %copy-start.2 = (bf16[2,512,4,128]{1,0,3,2:T(2,128)(2,1)S(1)}, bf16[2,512,4,128]{1,0,3,2:T(2,128)(2,1)}, u32[]{:S(2)}) copy-start(bf16[2,512,4,128]{1,0,3,2:T(2,128)(2,1)} %convert_element_type.24) | copy-start | bytes 3145732
  226.3 0.7 copy-start
Sparse Core Ops, SparseCore 0:
  9.2 85.7 all-gather.7
  97.8 88.0 all-gather.5
  227.1 96.5 all-gather.9
where the time goes:
time: 449 us; the launch traced here: 447 us
  waiting for transfers between devices  176 us (39%)
  blocking collectives  125 us (28%)
  other arithmetic  76.6 us (17%)
  matrix products  27.7 us (6%)
  local copies, waits for them, and re-layouts  26.2 us (6%)
  between operations  13.9 us (3%)
    unnamed x1, blocking collectives  125 us
    all_gather x1, waiting for transfers between devices, on_device(): lax.all_gather(projection, 'seq', axis=1, tiled=True)  90.9 us
    all_gather x1, waiting for transfers between devices, on_device(): features = lax.all_gather(tokens, 'fsdp', axis=1, tiled=True)  83.5 us
    add x63, other arithmetic, combine(): later[0][:, None, None] * earlier[1] + later[1]  66.8 us
    dot_general x1, matrix products, on_device(): jnp.einsum('td,cdn->ctn', features, lax.all_gather(projection, 'seq', axi...  17.3 us
  transfers between devices with their start and end apart: 3, of which 2 were waited for; matrix products, arithmetic and copies ran while one was open for 1% of the time, Pallas kernels for 0%

commit v1 on v0

--- a/solution.py
+++ b/solution.py
@@ -2,6 +2,7 @@
 import jax.numpy as jnp
 from jax import lax
 from jax.sharding import PartitionSpec as P
+from jax.lax import axis_index, axis_size, ppermute
 
 BLK = 512
 
@@ -71,7 +72,20 @@
 
 
 def on_device(tokens, projection, log_decay):
-    features = lax.all_gather(tokens, "fsdp", axis=1, tiled=True)
+
+    def time_quotas_on_mesh(in_array, which_dim, peer_axis):
+        n_blocks = axis_size(peer_axis)
+        tmp = [None] * n_blocks
+        tmp[n_blocks - 1] = in_array
+        buffer = [(w, (w + 1) % n_blocks) for w in range(n_blocks)]
+        for c in range(n_blocks - 2, -1, -1):
+            tmp[c] = ppermute(tmp[c + 1], axis_name=peer_axis, perm=buffer)
+        after = jnp.concatenate(tmp, axis=which_dim)
+        z = axis_index(peer_axis)
+        v1 = (z + 1) * in_array.shape[which_dim]
+        return jnp.roll(after, v1, axis=which_dim)
+
+    features = time_quotas_on_mesh(tokens, 1, peer_axis="fsdp")
     rows = features.shape[0]
     heads = log_decay.shape[1]
     width = projection.shape[2]

time: 449 us -> 428 us (0.953)
  waiting for transfers between devices: 176 us -> 136 us
  local copies, waits for them, and re-layouts: 26.2 us -> 38.6 us
    ppermute x0 -> x3, waiting for transfers between devices: none -> 136 us  [time_quotas_on_mesh(): tmp[c] = ppermute(tmp[c + 1], axis_name=peer_axis, perm=buffer)]
    all_gather x1, waiting for transfers between devices: 90.9 us -> 0.01 us  [on_device(): lax.all_gather(projection, 'seq', axis=1, tiled=True)]
    all_gather x1 -> x0, waiting for transfers between devices: 83.5 us -> none  [on_device(): features = lax.all_gather(tokens, 'fsdp', axis=1, tiled=True)]
    unnamed x18 -> x23, local copies, waits for them, and re-layouts: 3.8 us -> 21.8 us
    squeeze x2 -> x1, local copies, waits for them, and re-layouts: 8.14 us -> 1.93 us  [on_device(): query_raw = raw[0]]
  transfers between devices with their start and end apart: 3 -> 5, of which waited for: 2 -> 3; matrix products, arithmetic and copies ran while one was open for 1% -> 6% of each run, Pallas kernels for 0% -> 0%
where the time goes in v1:
time: 428 us; the launch traced here: 425 us
  waiting for transfers between devices  136 us (32%)
  blocking collectives  125 us (29%)
  other arithmetic  78.8 us (18%)
  local copies, waits for them, and re-layouts  38.6 us (9%)
  matrix products  28.8 us (7%)
  between operations  14.2 us (3%)
    ppermute x3, waiting for transfers between devices, time_quotas_on_mesh(): tmp[c] = ppermute(tmp[c + 1], axis_name=peer_axis, perm=buffer)  136 us
    unnamed x1, blocking collectives  125 us
    add x63, other arithmetic, combine(): later[0][:, None, None] * earlier[1] + later[1]  66.8 us
    unnamed x23, local copies, waits for them, and re-layouts  21.8 us
    dot_general x1, matrix products, on_device(): jnp.einsum('td,cdn->ctn', features, lax.all_gather(projection, 'seq', axi...  16.4 us
  transfers between devices with their start and end apart: 5, of which 3 were waited for; matrix products, arithmetic and copies ran while one was open for 6% of the time, Pallas kernels for 0%

profile of v1, /device:TPU:249, one launch (start us, length us, event | category | flops | bytes accessed | tf_op | source)
XLA Modules:
  0.0 425.5 jit_solution(7310299068835257659)
XLA Ops:
  7.3 1.3 collective-permute-start
  8.6 46.7 %collective-permute-done = bf16[1024,1024]{1,0:T(8,128)(2,1)S(1)} collective-permute-done((bf16[1024,1024]{1,0:T(8,128)(2,1)}, bf16[1024,1024]{1,0:T(8,128)(2,1)S(1)}, u32[]{:S(2)}, u32[]{:S(2)}) %collective-permute-start) | collective-permute-done | bytes 2097184 | tf_op jit(solution)/shard_map/ppermute | solution.py:82
  55.3 46.9 %collective-permute-done.1 = bf16[1024,1024]{1,0:T(8,128)(2,1)} collective-permute-done((bf16[1024,1024]{1,0:T(8,128)(2,1)S(1)}, bf16[1024,1024]{1,0:T(8,128)(2,1)}, u32[]{:S(2)}, u32[]{:S(2)}) %collective-permute-start.1) | collective-permute-done | bytes 2097184 | tf_op jit(solution)/shard_map/ppermute | solution.py:82
  102.9 2.4 reduce-window.14
  106.3 42.1 %collective-permute-done.2 = bf16[1024,1024]{1,0:T(8,128)(2,1)} collective-permute-done((bf16[1024,1024]{1,0:T(8,128)(2,1)}, bf16[1024,1024]{1,0:T(8,128)(2,1)}, u32[]{:S(2)}, u32[]{:S(2)}) %collective-permute-start.2) | collective-permute-done | bytes 2097184 | tf_op jit(solution)/shard_map/ppermute | solution.py:82
  148.4 3.1 constant_dynamic-update-slice_fusion.8
  151.5 3.3 constant_dynamic-update-slice_fusion.7
  154.8 1.5 constant_dynamic-update-slice_fusion.6
  156.3 1.5 constant_dynamic-update-slice_fusion.5
  157.7 3.1 constant_dynamic-update-slice_fusion.4
  160.8 3.1 constant_dynamic-update-slice_fusion.3
  163.9 1.5 constant_dynamic-update-slice_fusion.2
  165.4 1.5 constant_dynamic-update-slice_fusion.1
  166.9 16.4 %fusion.27 = f32[3,1024,512]{2,1,0:T(8,128)S(1)} fusion(bf16[3,4096,512]{2,1,0:T(8,128)(2,1)} %all-gather.5.cloned.1.call-done, bf16[1024,8192]{1,0:T(8,128)(2,1)} %constant_dynamic-update-slice_fusion.1, s32[]{:T(128)S(6)} %select_n.25), kind=kOutput, calls=%fused_computation.40 | convolution fusion | flops 12884901888 | bytes 27262980 | tf_op jit(solution)/shard_map/td,cdn->ctn/dot_general | solution.py:99
  183.3 2.4 fusion.36
  185.7 1.1 slice.43
  186.8 1.9 squeeze.41
  188.7 2.9 squeeze.42
  191.6 1.3 convert_element_type.24
  193.0 3.7 multiply_convert_fusion.2
  197.6 2.7 fusion.30
  200.3 1.7 while.37
  204.2 124.6 %all-reduce = f32[256]{0:T(256)S(1)} all-reduce(f32[256]{0:T(256)S(1)} %exponential_dynamic-update-slice_fusion), channel_id=2, replica_groups=mesh['seq'=64,'fsdp'=4] {'seq'}, use_global_device_ids=true, to_apply=%add | all-reduce | flops 256 | bytes 2048
  329.0 69.8 %while.35 = (s32[]{:T(128)}, f32[4,128,128]{2,1,0:T(8,128)S(1)}, s32[]{:T(128)}, f32[64,4]{1,0:T(8,128)S(1)}, f32[64,4,128,128]{3,2,1,0:T(8,128)}, /*index=5*/s32[]{:T(128)}, s32[]{:T(128)}, s32[]{:T(128)}) while((s32[]{:T(128)}, f32[4,128,128]{2,1,0:T(8,128)S(1)}, s32[]{:T(128)}, f32[64,4]{1,0:T(8,128)S(1)}, f32[64,4,128,128]{3,2,1,0:T(8,128)}, ...), condition=%wide.region_7.8_spmd, body=%wide.region_6.7_spmd.sunk | while | flops 131077 | bytes 786607 | solution.py:20
  330.1 1.1 bitcast_add_fusion.4
  331.2 1.1 bitcast_add_fusion.4
  332.3 1.1 bitcast_add_fusion.4
  333.5 1.1 bitcast_add_fusion.4
  337.9 1.1 bitcast_add_fusion.4
  339.0 1.1 bitcast_add_fusion.4
  340.1 1.1 bitcast_add_fusion.4
  341.2 1.1 bitcast_add_fusion.4
  344.5 1.1 bitcast_add_fusion.4
  345.6 1.1 bitcast_add_fusion.4
  346.7 1.1 bitcast_add_fusion.4
  347.8 1.1 bitcast_add_fusion.4
  351.1 1.1 bitcast_add_fusion.4
  352.2 1.1 bitcast_add_fusion.4
  353.3 1.1 bitcast_add_fusion.4
  354.5 1.1 bitcast_add_fusion.4
  399.0 17.3 %while.36 = (s32[]{:T(128)}, bf16[2,512,4,128]{3,2,1,0:T(4,128)(2,1)}, bf16[2,512,4,128]{3,2,1,0:T(4,128)(2,1)S(1)}, f32[2,512,4]{1,2,0:T(4,128)S(1)}, bf16[2,51...) while((s32[]{:T(128)}, ...), condition=%wide.region_12.13_spmd, body=%wide.region_8.12_spmd.sunk | while | flops 945817664 | bytes 11955133 | solution.py:108
  399.0 1.2 reduce-window.24
  401.2 3.1 fusion.47
  404.4 1.8 multiply_reduce_fusion.2
  407.6 1.2 reduce-window.24
  409.9 3.1 fusion.47
  413.0 1.8 multiply_reduce_fusion.2
  416.2 2.4 copy.65
  (182 shorter events, 62.2 us)
Async XLA Ops:
  6.5 160.4 %all-gather.5.cloned.1.call-start = ((), (), s32[]{:S(2)}) async-start(), calls=%async_computation | async-start | bytes 12779520 | tf_op jit(solution)/shard_map/all_gather | solution.py:102
  7.3 321.7 %all-gather.7.cloned.1.call-start = ((), (), s32[]{:S(2)}) async-start(), calls=%async_computation.1 | async-start | bytes 17039360 | tf_op jit(solution)/shard_map/all_gather | solution.py:12
  7.3 48.0 %collective-permute-start = (bf16[1024,1024]{1,0:T(8,128)(2,1)}, bf16[1024,1024]{1,0:T(8,128)(2,1)S(1)}, u32[]{:S(2)}, u32[]{:S(2)}) collective-permute-start(bf16[1024,1024]{1,0:T(8,128)(2,1)} %param.9), channel_id=1, source_target_pairs={{0,1},{1,2},{2,3},{3,0},{4,5},{5,6},{6,7},{7,4},{8,9},{9,10},{10,1... | collective-permute-start | bytes 6291464 | tf_op jit(solution)/shard_map/ppermute | solution.py:82
  55.3 46.9 %collective-permute-start.1 = (bf16[1024,1024]{1,0:T(8,128)(2,1)S(1)}, bf16[1024,1024]{1,0:T(8,128)(2,1)}, u32[]{:S(2)}, u32[]{:S(2)}) collective-permute-start(bf16[1024,1024]{1,0:T(8,128)(2,1)S(1)} %collective-permute-done), channel_id=1, source_target_pairs={{0,1},{1,2},{2,3},{3,0},{4,5},{5,6},{6,7},{7,4},{8,9},{9,10},{10,1... | collective-permute-start | bytes 6291464 | tf_op jit(solution)/shard_map/ppermute | solution.py:82
  102.2 46.2 %collective-permute-start.2 = (bf16[1024,1024]{1,0:T(8,128)(2,1)}, bf16[1024,1024]{1,0:T(8,128)(2,1)}, u32[]{:S(2)}, u32[]{:S(2)}) collective-permute-start(bf16[1024,1024]{1,0:T(8,128)(2,1)} %collective-permute-done.1), channel_id=1, source_target_pairs={{0,1},{1,2},{2,3},{3,0},{4,5},{5,6},{6,7},{7,4},{8,9},{9,10},{10,1... | collective-permute-start | bytes 6291464 | tf_op jit(solution)/shard_map/ppermute | solution.py:82
  151.5 4.8 %copy-start.1 = (bf16[1024,1024]{1,0:T(8,128)(2,1)S(1)}, bf16[1024,1024]{1,0:T(8,128)(2,1)}, u32[]{:S(2)}) copy-start(bf16[1024,1024]{1,0:T(8,128)(2,1)} %param.9) | copy-start | bytes 6291460
  196.6 1.0 copy-start.2
  200.3 2.5 copy-start.5
  202.0 0.7 copy-start
  202.0 196.8 %copy-start.3 = (f32[2,4,128,128]{3,2,1,0:T(8,128)S(1)}, f32[2,4,128,128]{3,2,1,0:T(8,128)}, u32[]{:S(2)}) copy-start(f32[2,4,128,128]{3,2,1,0:T(8,128)} %get-tuple-element.114) | copy-start | bytes 1572868
  202.0 196.9 %copy-start.4 = (f32[1024,4]{0,1:T(4,128)S(1)}, f32[1024,4]{0,1:T(4,128)}, u32[]{:S(2)}) copy-start(f32[1024,4]{0,1:T(4,128)} %param.11) | copy-start | bytes 49156
Sparse Core Ops, SparseCore 0:
  10.2 87.1 all-gather.4
  202.9 97.1 all-gather.6
